TPU v7x, 32 devices: a whole 2x2x4 slice. The times are simulated.
32 devices in a mesh: dp: 8 (over z, x), mp: 4 (over y, core).
Axes of the slice: x: 2, y: 2, z: 4, core: 2. Of those that a mesh axis runs over, the one named last changes fastest.
Arguments:
- inputs: bfloat16 [3072, 8192], P('dp', 'mp'), may hold values from -6 to 6
- gate_preact: bfloat16 [3072, 28672], P('dp', 'mp'), may hold values from -6 to 6
- hidden_grad: bfloat16 [3072, 28672], P('dp', 'mp'), may hold values from -0.15625 to 0.15625
- projector: bfloat16 [8192, 512], P('mp'), may hold values from -0.0625 to 0.0625
- first_moment: float32 [28672, 512], P(('mp', 'dp')), may hold values from -0.6 to 0.6
- second_moment: float32 [28672, 512], P(('mp', 'dp')), may hold values from 0.01 to 0.1
Outputs:
- new_first: float32 [28672, 512], P(('mp', 'dp'))
- new_second: float32 [28672, 512], P(('mp', 'dp'))
- weight_update: bfloat16 [28672, 8192], P(('mp', 'dp'))
All inputs are finite; a program needn't handle non-finite values.
Results may differ from a plain program's by a relative error of at most 0.0058.
Values may be sent and summed in bfloat16 or wider, within the bound.
A program may use at most 128 MiB of HBM per device.

v0:
```python
import jax
import jax.numpy as jnp
from jax import lax
from jax.sharding import PartitionSpec as P


def local(inputs, gate_preact, hidden_grad, projector, first_moment, second_moment):
    grad_up = (
        hidden_grad.astype(jnp.float32) * jax.nn.silu(gate_preact.astype(jnp.float32))
    ).astype(jnp.bfloat16)
    full_proj = lax.all_gather(projector, "mp", axis=0, tiled=True)
    coord_sum = jnp.dot(
        lax.all_gather(inputs, "mp", axis=1, tiled=True),
        full_proj,
        preferred_element_type=jnp.float32,
    )
    coords = coord_sum.astype(jnp.bfloat16)
    all_coords = lax.all_gather(coords, "dp", axis=0, tiled=True)
    owner_cols = lax.all_to_all(grad_up, "dp", split_axis=1, concat_axis=0, tiled=True)
    projected = lax.dot_general(
        owner_cols, all_coords, (((0,), (0,)), ((), ())), preferred_element_type=jnp.float32
    )
    new_first = 0.9 * first_moment + 0.1 * projected
    new_second = 0.95 * second_moment + 0.05 * projected * projected
    direction = new_first / (1.0 - 0.81) / (jnp.sqrt(new_second / (1.0 - 0.9025)) + 1e-08)
    direction = direction.astype(jnp.bfloat16)
    update = 4.0 * lax.dot_general(
        direction, full_proj, (((1,), (1,)), ((), ())), preferred_element_type=jnp.float32
    )
    return (new_first, new_second, update.astype(jnp.bfloat16))


def solution(mesh):
    return jax.shard_map(
        local,
        mesh=mesh,
        in_specs=(
            P("dp", "mp"),
            P("dp", "mp"),
            P("dp", "mp"),
            P("mp", None),
            P(("mp", "dp"), None),
            P(("mp", "dp"), None),
        ),
        out_specs=(P(("mp", "dp"), None), P(("mp", "dp"), None), P(("mp", "dp"), None)),
        check_vma=False,
    )
```

profile of v0, /device:TPU:1, one launch (start us, length us, event | category | flops | bytes accessed | tf_op | source)
XLA Modules:
  0.0 240.0 jit_solution(7372738757020666787)
XLA Ops:
  7.2 0.0 all-gather.4.cloned.1.call-start
  7.2 0.7 all-gather.4.cloned.1.call-update
  7.9 0.0 all-gather.6.cloned.1.call-start
  7.9 0.7 all-gather.6.cloned.1.call-update
  8.6 8.3 %copy.10 = bf16[384,7168]{0,1:T(8,128)(2,1)} copy(bf16[384,7168]{1,0:T(8,128)(2,1)} %param.7) | data formatting | bytes 11010048 | tf_op args[1]
  16.9 8.4 %copy.9 = bf16[384,7168]{0,1:T(8,128)(2,1)} copy(bf16[384,7168]{1,0:T(8,128)(2,1)} %param.8) | data formatting | bytes 11010048 | tf_op args[2]
  25.3 8.8 %fusion.4 = bf16[384,7168]{0,1:T(8,128)(2,1)} fusion(bf16[384,7168]{0,1:T(8,128)(2,1)} %copy.10, bf16[384,7168]{0,1:T(8,128)(2,1)} %copy.9), kind=kLoop, calls=%fused_computation.7 | loop fusion | flops 22020096 | bytes 16515072 | tf_op jit(solution)/shard_map/convert_element_type | solution.py:10
  34.2 6.4 %all-to-all-start = ((bf16[384,8,896]{0,2,1:T(8,128)(2,1)}), bf16[384,8,896]{0,2,1:T(8,128)(2,1)}, u32[]{:S(2)}, u32[]{:S(2)}) async-start(bf16[384,8,896]{0,2,1:T(8,128)(2,1)} %bitcast.8), calls=%async_computation | async-start | bytes 11010048 | tf_op jit(solution)/shard_map/all_to_all | solution.py:19
  40.5 0.0 all-gather.8.cloned.1.call-start
  40.6 17.9 %all-gather.4.cloned.1.call-done = bf16[384,8192]{1,0:T(8,128)(2,1)} async-done(((bf16[384,2048]{1,0:T(8,128)(2,1)}), bf16[384,8192]{1,0:T(8,128)(2,1)}) %all-gather.4.cloned.1.call-update) | async-done | bytes 6291472 | tf_op jit(solution)/shard_map/all_gather | solution.py:13
  58.5 59.9 %all-gather.6.cloned.1.call-done = bf16[8192,512]{1,0:T(8,128)(2,1)} async-done(((bf16[2048,512]{1,0:T(8,128)(2,1)}), bf16[8192,512]{1,0:T(8,128)(2,1)}) %all-gather.6.cloned.1.call-update) | async-done | bytes 8388624 | tf_op jit(solution)/shard_map/all_gather | solution.py:11
  118.4 9.3 %convolution_convert_fusion = bf16[384,512]{1,0:T(8,128)(2,1)} fusion(bf16[384,8192]{1,0:T(8,128)(2,1)} %all-gather.4.cloned.1.call-done, bf16[8192,512]{1,0:T(8,128)(2,1)} %all-gather.6.cloned.1.call-done), kind=kOutput, calls=%fused_computation.12 | convolution fusion | flops 3221422080 | bytes 15073280 | tf_op jit(solution)/shard_map/dot_general | solution.py:12
  127.7 0.0 all-gather.8.cloned.1.call-update
  127.7 45.8 %all-to-all-done = bf16[384,8,896]{0,2,1:T(8,128)(2,1)} async-done(((bf16[384,8,896]{0,2,1:T(8,128)(2,1)}), bf16[384,8,896]{0,2,1:T(8,128)(2,1)}, u32[]{:S(2)}, u32[]{:S(2)}) %all-to-all-start) | async-done | bytes 5505056 | tf_op jit(solution)/shard_map/all_to_all | solution.py:19
  173.5 0.0 copy-start
  173.5 8.4 %copy.11 = bf16[8,384,896]{2,1,0:T(8,128)(2,1)} copy(bf16[8,384,896]{1,2,0:T(8,128)(2,1)} %bitcast.1) | data formatting | bytes 11010048 | tf_op jit(solution)/shard_map/all_to_all | solution.py:19
  182.0 26.8 %all-gather.8.cloned.1.call-done = bf16[3072,512]{1,0:T(8,128)(2,1)} async-done(((bf16[384,512]{1,0:T(8,128)(2,1)}), bf16[3072,512]{1,0:T(8,128)(2,1)}) %all-gather.8.cloned.1.call-update) | async-done | bytes 3145744 | tf_op jit(solution)/shard_map/all_gather | solution.py:18
  208.8 0.0 copy-done
  208.8 9.2 %fusion.5 = (f32[896,512]{1,0:T(8,128)}, f32[896,512]{1,0:T(8,128)}) fusion(f32[896,512]{1,0:T(8,128)S(1)} %copy-done, f32[896,512]{1,0:T(8,128)} %param.10, bf16[3072,896]{1,0:T(8,128)(2,1)} %bitcast.9, bf16[3072,512]{1,0:T(8,128)(2,1)} %all-gather.8.cloned.1.call-done), kind=kOutput, calls=%fused_computation.9 | convolution fusion | flops 2821783552 | bytes 15990784 | tf_op jit(solution)/shard_map/dot_general | solution.py:20
  218.0 15.5 %multiply_convert_fusion = bf16[896,8192]{1,0:T(8,128)(2,1)} fusion(bf16[8192,512]{1,0:T(8,128)(2,1)} %all-gather.6.cloned.1.call-done, f32[896,512]{1,0:T(8,128)} %get-tuple-element.3, f32[896,512]{1,0:T(8,128)} %get-tuple-element.4), kind=kOutput, calls=%fused_computation | convolution fusion | flops 7533166592 | bytes 26738688 | tf_op jit(solution)/shard_map/dot_general | solution.py:27
Async XLA Ops:
  7.2 51.3 %all-gather.4.cloned.1.call-start = ((), (), s32[]{:S(2)}) async-start(), calls=%async_computation.1 | async-start | bytes 7864320 | tf_op jit(solution)/shard_map/all_gather | solution.py:13
  7.9 110.5 %all-gather.6.cloned.1.call-start = ((), (), s32[]{:S(2)}) async-start(), calls=%async_computation.2 | async-start | bytes 10485760 | tf_op jit(solution)/shard_map/all_gather | solution.py:11
  34.2 139.4 %all-to-all-start = ((bf16[384,8,896]{0,2,1:T(8,128)(2,1)}), bf16[384,8,896]{0,2,1:T(8,128)(2,1)}, u32[]{:S(2)}, u32[]{:S(2)}) async-start(bf16[384,8,896]{0,2,1:T(8,128)(2,1)} %bitcast.8), calls=%async_computation | async-start | bytes 11010048 | tf_op jit(solution)/shard_map/all_to_all | solution.py:19
  40.5 168.3 %all-gather.8.cloned.1.call-start = ((), (), s32[]{:S(2)}) async-start(), calls=%async_computation.3 | async-start | bytes 3538944 | tf_op jit(solution)/shard_map/all_gather | solution.py:18
  173.5 35.3 %copy-start = (f32[896,512]{1,0:T(8,128)S(1)}, f32[896,512]{1,0:T(8,128)}, u32[]{:S(2)}) copy-start(f32[896,512]{1,0:T(8,128)} %param.11) | copy-start | bytes 5505028
Sparse Core Ops, SparseCore 0:
  9.6 48.8 all-gather.3
  60.0 58.2 all-gather.5
  127.9 80.8 all-gather.7
where the time goes:
time: 242 us; the launch traced here: 240 us
  waiting for transfers between devices  152 us (63%)
  matrix products  34 us (14%)
  local copies, waits for them, and re-layouts  25.1 us (10%)
  between operations  13.7 us (6%)
  other arithmetic  8.83 us (4%)
  starting transfers between devices  6.46 us (3%)
    all_gather x1, waiting for transfers between devices, local(): full_proj = lax.all_gather(projector, 'mp', axis=0, tiled=True)  59.9 us
    all_to_all x1, waiting for transfers between devices, local(): lax.all_to_all(grad_up, 'dp', split_axis=1, concat_axis=0, tiled=True)  45.8 us
    all_gather x1, waiting for transfers between devices, local(): all_coords = lax.all_gather(coords, 'dp', axis=0, tiled=True)  26.8 us
    all_gather x1, waiting for transfers between devices, local(): lax.all_gather(inputs, 'mp', axis=1, tiled=True)  17.9 us
    unnamed x4, local copies, waits for them, and re-layouts  16.7 us
    dot_general x1, matrix products, local(): lax.dot_general(direction, full_proj, (((1,), (1,)), ((), ())), preferred...  15.5 us
    dot_general x1, matrix products, local(): jnp.dot(lax.all_gather(inputs, 'mp', axis=1, tiled=True), full_proj, pref...  9.35 us
    dot_general x1, matrix products, local(): lax.dot_general(owner_cols, all_coords, (((0,), (0,)), ((), ())), preferr...  9.16 us
  transfers between devices with their start and end apart: 4, of which 4 were waited for; matrix products, arithmetic and copies ran while one was open for 18% of the time, Pallas kernels for 0%

commit v1 on v0

v1 whole, which is shorter than its diff:
```python
import functools

import jax
import jax.numpy as jnp
from jax import lax
from jax.experimental import pallas as pl
from jax.experimental.pallas import tpu as pltpu
from jax.sharding import PartitionSpec as P

MESH = pl.DeviceIdType.MESH
F32 = jnp.float32
BF16 = jnp.bfloat16


def dot_t(a, b):
    return lax.dot_general(a, b, (((0,), (0,)), ((), ())), preferred_element_type=F32)


def exchange_kernel(
    cfg, x_hbm, gate_hbm, hg_hbm, p_hbm, out_ref, pfull,
    xin, pin, gbuf, hbuf, gs, go, gr, ps, ru, rd, cpart, c1s, c1r, co, acc_ref,
    lsem, gsem, hsem, xs, xr, zs, zu, zd,
    s1s, s1r, s2s, s2r, sxs, sxr, s3s, s3r, sib_s, sib_r, pgs, pgr, pfs, pfr,
):
    n, mp, f, cw, pieces, sliced = cfg
    chunks = f // cw
    dp = lax.axis_index("dp")
    m = lax.axis_index("mp")
    z, x = dp // 2, dp % 2
    xp = dp + 1 - 2 * x
    core = m % 2
    sib = m + 1 - 2 * core
    chip = m // 2
    nch = mp // 2
    rows = co.shape[1] // mp
    pr = p_hbm.shape[0]
    pc_rows = pr // pieces

    def peer(o):
        return lax.rem(m + o, mp)

    def source(o):
        return lax.rem(m + mp - o, mp)

    def blocks(fn_up, fn_down, fn_own):
        @pl.loop(0, n - 1)
        def _(k):
            @pl.when(k >= z)
            def _():
                fn_up(n - 1 - k + z)

            @pl.when(k >= n - 1 - z)
            def _():
                fn_down(k - (n - 1 - z))

        if fn_own is not None:
            fn_own(z)

    def cols(ref, d):
        if sliced:
            return ref.at[:, pl.ds(pl.multiple_of(d * f, 128), f)]
        return ref.at[d]

    def load(side, t):
        d = 2 * t + (x if side else 1 - x)
        return (
            pltpu.make_async_copy(cols(gate_hbm, d), gbuf.at[side, t], gsem.at[side, t]),
            pltpu.make_async_copy(cols(hg_hbm, d), hbuf.at[side, t], hsem.at[side, t]),
        )

    def start_load(side):
        def go_(t):
            for c in load(side, t):
                c.start()
        return go_

    in_copy = pltpu.make_async_copy(x_hbm, xin, lsem.at[0])
    pin_copy = pltpu.make_async_copy(p_hbm, pin, lsem.at[1])
    my_rows = pl.ds(pl.multiple_of(m * pr, 16), pr)
    pown = pltpu.make_async_copy(p_hbm, pfull.at[my_rows], lsem.at[2])
    in_copy.start()
    pin_copy.start()
    blocks(start_load(0), start_load(0), start_load(0))
    blocks(start_load(1), start_load(1), start_load(1))
    pown.start()

    bar = pltpu.get_barrier_semaphore()
    for o in range(1, mp):
        pl.semaphore_signal(bar, inc=1, device_id=(dp, peer(o)), device_id_type=MESH)
    pl.semaphore_signal(bar, inc=1, device_id=(xp, m), device_id_type=MESH)

    @pl.when(z > 0)
    def _():
        pl.semaphore_signal(bar, inc=1, device_id=(dp - 2, m), device_id_type=MESH)

    @pl.when(z < n - 1)
    def _():
        pl.semaphore_signal(bar, inc=1, device_id=(dp + 2, m), device_id_type=MESH)

    in_copy.wait()
    pin_copy.wait()

    @pl.loop(0, mp)
    def _(q):
        r = pl.ds(pl.multiple_of(q * rows, 16), rows)
        v = jnp.dot(xin[r, :], pin[...], preferred_element_type=F32)
        cpart[q] = v
        c1s[q] = v.astype(BF16)

    neighbours = (z + n - 1) // n + (2 * n - 2 - z) // n
    pl.semaphore_wait(bar, mp + neighbours)

    def rc(src, dst, ss, rs, dev):
        return pltpu.make_async_remote_copy(
            src_ref=src, dst_ref=dst, send_sem=ss, recv_sem=rs, device_id=dev, device_id_type=MESH
        )

    def first(o):
        return rc(c1s.at[peer(o)], c1r.at[o - 1], s1s.at[o - 1], s1r.at[o - 1], (dp, peer(o)))

    for o in range(1, mp):
        first(o).start()

    def grad(side, t, c):
        sl = pl.ds(pl.multiple_of(c * cw, 128), cw) if chunks > 1 else slice(None)
        v = gbuf[side, t, :, sl].astype(F32)
        h = 0.5 * v
        silu = h + h * jnp.tanh(h)
        return (hbuf[side, t, :, sl].astype(F32) * silu).astype(BF16)

    def xcopy(t, c):
        return rc(gs.at[t, c], gr.at[t, c], xs.at[t, c], xr.at[t, c], (xp, m))

    def send_grads(t):
        for c in load(0, t):
            c.wait()

        @pl.loop(0, chunks)
        def _(c):
            gs[t, c] = grad(0, t, c)
            xcopy(t, c).start()

    def own_grads(t):
        for c in load(1, t):
            c.wait()

        @pl.loop(0, chunks)
        def _(c):
            go[t, c] = grad(1, t, c)

    blocks(send_grads, send_grads, None)

    def crow(q):
        return pl.ds(pl.multiple_of(q * rows, 16), rows)

    def second(o, q):
        return rc(co.at[0, crow(q)], co.at[0, crow(q)], s2s.at[o - 1], s2r.at[o - 1], (dp, peer(o)))

    def third(o, q):
        return rc(co.at[1, crow(q)], co.at[1, crow(q)], s3s.at[o - 1], s3r.at[o - 1], (dp, peer(o)))

    across = rc(co.at[0, crow(m)], co.at[1, crow(m)], sxs.at[0], sxr.at[0], (xp, m))

    total = cpart[m]
    for o in range(1, mp):
        first(o).wait_recv()
        total = total + c1r[o - 1].astype(F32)
    co[0, crow(m), :] = total.astype(BF16)
    across.start()
    for o in range(1, mp):
        second(o, m).start()

    send_grads(z)
    across.wait_recv()
    for o in range(1, mp):
        third(o, m).start()

    def piece(q, i):
        return pfull.at[pl.ds(pl.multiple_of(q * pr + i * pc_rows, 16), pc_rows)]

    sib_copy = rc(p_hbm, pfull.at[my_rows], sib_s.at[0], sib_r.at[0], (dp, sib))

    def chip_peer(o):
        return lax.rem(chip + o, nch) * 2 + core

    def chip_source(o, c):
        return lax.rem(chip + nch - o, nch) * 2 + c

    def pg(o, i):
        src = p_hbm.at[pl.ds(i * pc_rows, pc_rows)]
        return rc(src, piece(m, i), pgs.at[o - 1, i], pgr.at[o - 1, i], (dp, chip_peer(o)))

    def pg_in(o, i):
        q = chip_source(o, core)
        return rc(piece(q, i), piece(q, i), pgs.at[o - 1, i], pgr.at[o - 1, i], (dp, q))

    def pf(o, i, c):
        q = chip_source(o, c)
        return rc(piece(q, i), piece(q, i), pfs.at[o - 1, i], pfr.at[o - 1, i], (dp, sib))

    for o in range(1, nch):
        for i in range(pieces):
            pg(o, i).start()
    sib_copy.start()

    blocks(own_grads, own_grads, own_grads)
    for o in range(1, mp):
        second(o, source(o)).wait_recv()
        third(o, source(o)).wait_recv()

    def partial(t, c):
        xcopy(t, c).wait_recv()
        return dot_t(go[t, c], co[0]) + dot_t(gr[t, c], co[1])

    def zup(t, c):
        return rc(ps.at[t, c], ru.at[t, c], zs.at[t, c], zu.at[t, c], (dp + 2, m))

    def zdown(t, c):
        return rc(ps.at[t, c], rd.at[t, c], zs.at[t, c], zd.at[t, c], (dp - 2, m))

    def zup_in(t, c):
        return rc(ps.at[t, c], ru.at[t, c], zs.at[t, c], zu.at[t, c], (dp - 2, m))

    def zdown_in(t, c):
        return rc(ps.at[t, c], rd.at[t, c], zs.at[t, c], zd.at[t, c], (dp + 2, m))

    def reduce_up(t):
        @pl.loop(0, chunks)
        def _(c):
            acc_ref[...] = partial(t, c)

            @pl.when(z > 0)
            def _():
                zup_in(t, c).wait_recv()
                acc_ref[...] += ru[t, c].astype(F32)

            ps[t, c] = acc_ref[...].astype(BF16)
            zup(t, c).start()

    def reduce_down(t):
        @pl.loop(0, chunks)
        def _(c):
            acc_ref[...] = partial(t, c)

            @pl.when(z < n - 1)
            def _():
                zdown_in(t, c).wait_recv()
                acc_ref[...] += rd[t, c].astype(F32)

            ps[t, c] = acc_ref[...].astype(BF16)
            zdown(t, c).start()

    blocks(reduce_up, reduce_down, None)

    def orow(c):
        return pl.ds(pl.multiple_of(c * cw, 16), cw)

    @pl.loop(0, chunks)
    def _(c):
        out_ref[orow(c), :] = partial(z, c)

    for o in range(1, nch):
        for i in range(pieces):
            pg_in(o, i).wait_recv()
            pf(o, i, core).start()

    @pl.loop(0, chunks)
    def _(c):
        @pl.when(z > 0)
        def _():
            zup_in(z, c).wait_recv()
            out_ref[orow(c), :] += ru[z, c].astype(F32)

        @pl.when(z < n - 1)
        def _():
            zdown_in(z, c).wait_recv()
            out_ref[orow(c), :] += rd[z, c].astype(F32)

    pown.wait()
    sib_copy.wait_send()
    rc(p_hbm, pfull.at[pl.ds(pl.multiple_of(sib * pr, 16), pr)],
       sib_s.at[0], sib_r.at[0], (dp, sib)).wait_recv()
    for o in range(1, nch):
        for i in range(pieces):
            pg(o, i).wait_send()
            pf(o, i, core).wait_send()
            pf(o, i, 1 - core).wait_recv()
    across.wait_send()
    for o in range(1, mp):
        first(o).wait_send()
        second(o, m).wait_send()
        third(o, m).wait_send()

    def finish_x(t):
        @pl.loop(0, chunks)
        def _(c):
            xcopy(t, c).wait_send()

    def finish_up(t):
        finish_x(t)

        @pl.loop(0, chunks)
        def _(c):
            zup(t, c).wait_send()

    def finish_down(t):
        finish_x(t)

        @pl.loop(0, chunks)
        def _(c):
            zdown(t, c).wait_send()

    blocks(finish_up, finish_down, finish_x)


def adam_kernel(proj_ref, m_ref, v_ref, p_ref, nm_ref, nv_ref, u_ref, d_ref):
    @pl.when(pl.program_id(0) == 0)
    def _():
        g = proj_ref[...]
        nm = 0.9 * m_ref[...] + 0.1 * g
        nv = 0.95 * v_ref[...] + 0.05 * g * g
        nm_ref[...] = nm
        nv_ref[...] = nv
        d = nm / (1.0 - 0.81) / (jnp.sqrt(nv / (1.0 - 0.9025)) + 1e-08)
        d_ref[...] = d.astype(BF16)

    u = lax.dot_general(
        d_ref[...], p_ref[...], (((1,), (1,)), ((), ())), preferred_element_type=F32
    )
    u_ref[...] = (4.0 * u).astype(BF16)


def local(ndp, mp, inputs, gate, hg, projector, first_moment, second_moment):
    tok, dl = inputs.shape
    units = gate.shape[1]
    pr, rank = projector.shape
    n = ndp // 2
    f = units // ndp
    sliced = f % 128 == 0
    cw = 128 if sliced else f
    chunks = f // cw
    pieces = 4
    if not sliced:
        gate = gate.reshape(tok, ndp, f).transpose(1, 0, 2)
        hg = hg.reshape(tok, ndp, f).transpose(1, 0, 2)
    rows = tok // mp
    any_ = pl.BlockSpec(memory_space=pl.ANY)
    dma = pltpu.SemaphoreType.DMA
    nch1 = max(mp // 2 - 1, 1)
    projected, pfull = pl.pallas_call(
        functools.partial(exchange_kernel, (n, mp, f, cw, pieces, sliced)),
        out_shape=(
            jax.ShapeDtypeStruct((f, rank), F32),
            jax.ShapeDtypeStruct((pr * mp, rank), BF16),
        ),
        in_specs=[any_] * 4,
        out_specs=(pl.BlockSpec(memory_space=pltpu.VMEM), any_),
        scratch_shapes=[
            pltpu.VMEM((tok, dl), BF16),
            pltpu.VMEM((pr, rank), BF16),
            pltpu.VMEM((2, n, tok, f), BF16),
            pltpu.VMEM((2, n, tok, f), BF16),
            pltpu.VMEM((n, chunks, tok, cw), BF16),
            pltpu.VMEM((n, chunks, tok, cw), BF16),
            pltpu.VMEM((n, chunks, tok, cw), BF16),
            pltpu.VMEM((n, chunks, cw, rank), BF16),
            pltpu.VMEM((n, chunks, cw, rank), BF16),
            pltpu.VMEM((n, chunks, cw, rank), BF16),
            pltpu.VMEM((mp, rows, rank), F32),
            pltpu.VMEM((mp, rows, rank), BF16),
            pltpu.VMEM((mp - 1, rows, rank), BF16),
            pltpu.VMEM((2, tok, rank), BF16),
            pltpu.VMEM((cw, rank), F32),
            dma((3,)),
            dma((2, n)), dma((2, n)),
            dma((n, chunks)), dma((n, chunks)),
            dma((n, chunks)), dma((n, chunks)), dma((n, chunks)),
            dma((mp - 1,)), dma((mp - 1,)),
            dma((mp - 1,)), dma((mp - 1,)),
            dma((1,)), dma((1,)),
            dma((mp - 1,)), dma((mp - 1,)),
            dma((1,)), dma((1,)),
            dma((nch1, pieces)), dma((nch1, pieces)),
            dma((nch1, pieces)), dma((nch1, pieces)),
        ],
        compiler_params=pltpu.CompilerParams(
            collective_id=0, has_side_effects=True, vmem_limit_bytes=56 * 2**20
        ),
        cost_estimate=pl.CostEstimate(
            flops=2 * tok * dl * rank + 2 * tok * units * rank,
            bytes_accessed=4 * tok * units + 2 * tok * dl + 2 * pr * rank * mp,
            transcendentals=tok * units,
        ),
        name="exchange",
    )(inputs, gate, hg, projector)

    d = pr * mp
    bw = 1024 if d % 1024 == 0 else d
    full = pl.BlockSpec((f, rank), lambda i: (0, 0))
    return pl.pallas_call(
        adam_kernel,
        grid=(d // bw,),
        out_shape=(
            jax.ShapeDtypeStruct((f, rank), F32),
            jax.ShapeDtypeStruct((f, rank), F32),
            jax.ShapeDtypeStruct((f, d), BF16),
        ),
        in_specs=[full, full, full, pl.BlockSpec((bw, rank), lambda i: (i, 0))],
        out_specs=(full, full, pl.BlockSpec((f, bw), lambda i: (0, i))),
        scratch_shapes=[pltpu.VMEM((f, rank), BF16)],
        compiler_params=pltpu.CompilerParams(vmem_limit_bytes=48 * 2**20),
        name="update",
    )(projected, first_moment, second_moment, pfull)


def solution(mesh):
    return jax.shard_map(
        functools.partial(local, mesh.shape["dp"], mesh.shape["mp"]),
        mesh=mesh,
        in_specs=(
            P("dp", "mp"),
            P("dp", "mp"),
            P("dp", "mp"),
            P("mp", None),
            P(("mp", "dp"), None),
            P(("mp", "dp"), None),
        ),
        out_specs=(P(("mp", "dp"), None), P(("mp", "dp"), None), P(("mp", "dp"), None)),
        check_vma=False,
    )
```

time: 242 us -> 145 us (0.60)
  waiting for transfers between devices: 152 us -> 0 us
  Pallas kernels: 0 us -> 143 us
  matrix products: 34 us -> 0 us
  local copies, waits for them, and re-layouts: 25.1 us -> 1.5 us
  between operations: 13.7 us -> 0.68 us
  other arithmetic: 8.83 us -> 0 us
  starting transfers between devices: 6.46 us -> 0 us
    pallas_call x0 -> x2, Pallas kernels: none -> 143 us  [the longest x1 126 us: local(): pl.pallas_call(functools.partial(exchange_kernel, (n, mp, f, cw, pieces,...]
    all_gather x3 -> x0, waiting for transfers between devices: 105 us -> none  [the longest x1 59.9 us: local(): full_proj = lax.all_gather(projector, 'mp', axis=0, tiled=True)]
    all_to_all x1 -> x0, waiting for transfers between devices: 45.8 us -> none  [local(): lax.all_to_all(grad_up, 'dp', split_axis=1, concat_axis=0, tiled=True)]
    dot_general x3 -> x0, matrix products: 34 us -> none  [the longest x1 15.5 us: local(): lax.dot_general(direction, full_proj, (((1,), (1,)), ((), ())), preferred...]
    unnamed x4 -> x6, local copies, waits for them, and re-layouts: 16.7 us -> 1.5 us
    convert_element_type x1 -> x0, other arithmetic: 8.83 us -> none  [local(): grad_up = (hidden_grad.astype(jnp.float32) * jax.nn.silu(gate_preact.asty...]
    all_to_all x1 -> x0, local copies, waits for them, and re-layouts: 8.42 us -> none  [local(): lax.all_to_all(grad_up, 'dp', split_axis=1, concat_axis=0, tiled=True)]
    all_to_all x1 -> x0, starting transfers between devices: 6.35 us -> none  [local(): lax.all_to_all(grad_up, 'dp', split_axis=1, concat_axis=0, tiled=True)]
  transfers between devices with their start and end apart: 4 -> 0, of which waited for: 4 -> 0; matrix products, arithmetic and copies ran while one was open for 18% -> 0% of each run, Pallas kernels for 0% -> 0%
where the time goes in v1:
time: 145 us
  Pallas kernels  143 us (99%)
  local copies, waits for them, and re-layouts  1.5 us (1%)
    pallas_call x1, Pallas kernels, local(): pl.pallas_call(functools.partial(exchange_kernel, (n, mp, f, cw, pieces,...  126 us
    pallas_call x1, Pallas kernels, local(): pl.pallas_call(adam_kernel, grid=(d // bw,), out_shape=(jax.ShapeDtypeStr...  16.3 us

profile of v1, /device:TPU:1, one launch (start us, length us, event | category | flops | bytes accessed | tf_op | source)
XLA Modules:
  0.0 144.9 jit_solution(10535759186603144560)
XLA Ops:
  0.6 0.0 copy-start.1
  0.6 0.0 copy-start
  0.7 126.4 %exchange.1 = (f32[896,512]{1,0:T(8,128)}, bf16[8192,512]{1,0:T(8,128)(2,1)}) custom-call(bf16[384,2048]{1,0:T(8,128)(2,1)} %x_hbm.1, bf16[384,7168]{1,0:T(8,128)(2,1)} %gate_hbm.1, bf16[384,7168]{1,0:T(8,128)(2,1)} %hg_hbm.1, bf16[2048,512]{1,0:T(8,128)(2,1)} %p_hbm.1), custom_call_target="tpu_custom_call" | custom-call | flops 3623878656 | bytes 20971520 | tf_op jit(solution)/shard_map/exchange/pallas_call | solution.py:350
  127.0 0.0 copy-done.1
  127.0 0.0 copy-done
  127.1 0.0 copy-start.2
  127.1 1.5 %copy-done.2 = f32[896,512]{1,0:T(8,128)S(1)} copy-done((f32[896,512]{1,0:T(8,128)S(1)}, f32[896,512]{1,0:T(8,128)}, u32[]{:S(2)}) %copy-start.2) | copy-done | bytes 1835032
  128.6 16.3 %update.1 = (f32[896,512]{1,0:T(8,128)}, f32[896,512]{1,0:T(8,128)}, bf16[896,8192]{1,0:T(8,128)(2,1)}) custom-call(f32[896,512]{1,0:T(8,128)S(1)} %copy-done.2, f32[896,512]{1,0:T(8,128)S(1)} %copy-done, f32[896,512]{1,0:T(8,128)S(1)} %copy-done.1, bf16[8192,512]{1,0:T(8,128)(2,1)} %get-tuple-element.6.p_ref), custom_call_target="tpu_custom_call" | custom-call | tf_op jit(solution)/shard_map/update/pallas_call | solution.py:400
Async XLA Ops:
  0.6 126.4 %copy-start.1 = (f32[896,512]{1,0:T(8,128)S(1)}, f32[896,512]{1,0:T(8,128)}, u32[]{:S(2)}) copy-start(f32[896,512]{1,0:T(8,128)} %v_ref.1) | copy-start | bytes 5505028
  0.6 126.4 %copy-start = (f32[896,512]{1,0:T(8,128)S(1)}, f32[896,512]{1,0:T(8,128)}, u32[]{:S(2)}) copy-start(f32[896,512]{1,0:T(8,128)} %m_ref.1) | copy-start | bytes 5505028
  127.1 1.5 %copy-start.2 = (f32[896,512]{1,0:T(8,128)S(1)}, f32[896,512]{1,0:T(8,128)}, u32[]{:S(2)}) copy-start(f32[896,512]{1,0:T(8,128)} %get-tuple-element.5.proj_ref) | copy-start | bytes 5505028

commit v2 on v1

--- a/solution.py
+++ b/solution.py
@@ -77,12 +77,11 @@
     in_copy = pltpu.make_async_copy(x_hbm, xin, lsem.at[0])
     pin_copy = pltpu.make_async_copy(p_hbm, pin, lsem.at[1])
     my_rows = pl.ds(pl.multiple_of(m * pr, 16), pr)
-    pown = pltpu.make_async_copy(p_hbm, pfull.at[my_rows], lsem.at[2])
+    pown = pltpu.make_async_copy(pin, pfull.at[my_rows], lsem.at[2])
     in_copy.start()
     pin_copy.start()
     blocks(start_load(0), start_load(0), start_load(0))
     blocks(start_load(1), start_load(1), start_load(1))
-    pown.start()
 
     bar = pltpu.get_barrier_semaphore()
     for o in range(1, mp):
@@ -99,6 +98,7 @@
 
     in_copy.wait()
     pin_copy.wait()
+    pown.start()
 
     @pl.loop(0, mp)
     def _(q):
@@ -138,7 +138,6 @@
         @pl.loop(0, chunks)
         def _(c):
             gs[t, c] = grad(0, t, c)
-            xcopy(t, c).start()
 
     def own_grads(t):
         for c in load(1, t):
@@ -148,7 +147,22 @@
         def _(c):
             go[t, c] = grad(1, t, c)
 
-    blocks(send_grads, send_grads, None)
+    upper = 2 * z // n
+    lead = (1 - 2 * upper) * (n - 1 - 2 * z)
+
+    def order(j):
+        alone = (lead + n - 1 - j) // n
+        r = (j - lead) * (1 - alone)
+        half, odd = r // 2, r % 2
+        low = alone * (n - 1 - j) + (1 - alone) * ((1 - odd) * (2 * z - half) + odd * half)
+        high = alone * j + (1 - alone) * ((1 - odd) * (n - 1 - half) + odd * (lead + half))
+        return (1 - upper) * low + upper * high
+
+    send_grads(order(0))
+
+    @pl.loop(0, chunks)
+    def _(c):
+        xcopy(order(0), c).start()
 
     def crow(q):
         return pl.ds(pl.multiple_of(q * rows, 16), rows)
@@ -170,7 +184,10 @@
     for o in range(1, mp):
         second(o, m).start()
 
-    send_grads(z)
+    @pl.loop(1, n)
+    def _(j):
+        send_grads(order(j))
+
     across.wait_recv()
     for o in range(1, mp):
         third(o, m).start()
@@ -208,8 +225,10 @@
         second(o, source(o)).wait_recv()
         third(o, source(o)).wait_recv()
 
-    def partial(t, c):
+    def partial(t, c, following=None):
         xcopy(t, c).wait_recv()
+        if following is not None:
+            xcopy(following, c).start()
         return dot_t(go[t, c], co[0]) + dot_t(gr[t, c], co[1])
 
     def zup(t, c):
@@ -224,10 +243,10 @@
     def zdown_in(t, c):
         return rc(ps.at[t, c], rd.at[t, c], zs.at[t, c], zd.at[t, c], (dp + 2, m))
 
-    def reduce_up(t):
-        @pl.loop(0, chunks)
-        def _(c):
-            acc_ref[...] = partial(t, c)
+    def reduce_up(t, following):
+        @pl.loop(0, chunks)
+        def _(c):
+            acc_ref[...] = partial(t, c, following)
 
             @pl.when(z > 0)
             def _():
@@ -237,10 +256,10 @@
             ps[t, c] = acc_ref[...].astype(BF16)
             zup(t, c).start()
 
-    def reduce_down(t):
-        @pl.loop(0, chunks)
-        def _(c):
-            acc_ref[...] = partial(t, c)
+    def reduce_down(t, following):
+        @pl.loop(0, chunks)
+        def _(c):
+            acc_ref[...] = partial(t, c, following)
 
             @pl.when(z < n - 1)
             def _():
@@ -250,7 +269,17 @@
             ps[t, c] = acc_ref[...].astype(BF16)
             zdown(t, c).start()
 
-    blocks(reduce_up, reduce_down, None)
+    @pl.loop(0, n - 1)
+    def _(j):
+        t, following = order(j), order(j + 1)
+
+        @pl.when(t > z)
+        def _():
+            reduce_up(t, following)
+
+        @pl.when(t < z)
+        def _():
+            reduce_down(t, following)
 
     def orow(c):
         return pl.ds(pl.multiple_of(c * cw, 16), cw)

time: 145 us -> 115 us (0.79)
  Pallas kernels: 143 us -> 113 us
    pallas_call x1, Pallas kernels: 126 us -> 96.5 us  [local(): pl.pallas_call(functools.partial(exchange_kernel, (n, mp, f, cw, pieces,...]
where the time goes in v2:
time: 115 us
  Pallas kernels  113 us (98%)
  local copies, waits for them, and re-layouts  1.5 us (1%)
    pallas_call x1, Pallas kernels, local(): pl.pallas_call(functools.partial(exchange_kernel, (n, mp, f, cw, pieces,...  96.5 us
    pallas_call x1, Pallas kernels, local(): pl.pallas_call(adam_kernel, grid=(d // bw,), out_shape=(jax.ShapeDtypeStr...  16.3 us

profile of v2, /device:TPU:1, one launch (start us, length us, event | category | flops | bytes accessed | tf_op | source)
XLA Modules:
  0.0 115.0 jit_solution(11566279773783727490)
XLA Ops:
  0.6 0.0 copy-start.1
  0.6 0.0 copy-start
  0.7 96.5 %exchange.1 = (f32[896,512]{1,0:T(8,128)}, bf16[8192,512]{1,0:T(8,128)(2,1)}) custom-call(bf16[384,2048]{1,0:T(8,128)(2,1)} %x_hbm.1, bf16[384,7168]{1,0:T(8,128)(2,1)} %gate_hbm.1, bf16[384,7168]{1,0:T(8,128)(2,1)} %hg_hbm.1, bf16[2048,512]{1,0:T(8,128)(2,1)} %p_hbm.1), custom_call_target="tpu_custom_call" | custom-call | flops 3623878656 | bytes 20971520 | tf_op jit(solution)/shard_map/exchange/pallas_call | solution.py:379
  97.1 0.0 copy-done.1
  97.1 0.0 copy-done
  97.1 0.0 copy-start.2
  97.1 1.5 %copy-done.2 = f32[896,512]{1,0:T(8,128)S(1)} copy-done((f32[896,512]{1,0:T(8,128)S(1)}, f32[896,512]{1,0:T(8,128)}, u32[]{:S(2)}) %copy-start.2) | copy-done | bytes 1835032
  98.6 16.3 %update.1 = (f32[896,512]{1,0:T(8,128)}, f32[896,512]{1,0:T(8,128)}, bf16[896,8192]{1,0:T(8,128)(2,1)}) custom-call(f32[896,512]{1,0:T(8,128)S(1)} %copy-done.2, f32[896,512]{1,0:T(8,128)S(1)} %copy-done, f32[896,512]{1,0:T(8,128)S(1)} %copy-done.1, bf16[8192,512]{1,0:T(8,128)(2,1)} %get-tuple-element.6.p_ref), custom_call_target="tpu_custom_call" | custom-call | tf_op jit(solution)/shard_map/update/pallas_call | solution.py:429
Async XLA Ops:
  0.6 96.5 %copy-start.1 = (f32[896,512]{1,0:T(8,128)S(1)}, f32[896,512]{1,0:T(8,128)}, u32[]{:S(2)}) copy-start(f32[896,512]{1,0:T(8,128)} %v_ref.1) | copy-start | bytes 5505028
  0.6 96.5 %copy-start = (f32[896,512]{1,0:T(8,128)S(1)}, f32[896,512]{1,0:T(8,128)}, u32[]{:S(2)}) copy-start(f32[896,512]{1,0:T(8,128)} %m_ref.1) | copy-start | bytes 5505028
  97.1 1.5 %copy-start.2 = (f32[896,512]{1,0:T(8,128)S(1)}, f32[896,512]{1,0:T(8,128)}, u32[]{:S(2)}) copy-start(f32[896,512]{1,0:T(8,128)} %get-tuple-element.5.proj_ref) | copy-start | bytes 5505028
